TPU v7x, 32 devices: a whole 2x2x4 slice. The times are simulated.
32 devices in a mesh: member: 16 (over z, y, core), tile: 2 (over x).
Axes of the slice: x: 2, y: 2, z: 4, core: 2. Of those that a mesh axis runs over, the one named last changes fastest.
Arguments:
- ensemble: float32 [64, 128, 2048], P('member', 'tile'), may hold values from -6 to 6
- velocity: float32 [2, 128, 2048], P(None, 'tile'), may hold values from -0.45 to 0.45
- observed_column: int32 [128, 16, 32], P('tile', 'member'), may hold values from 0 to 127
- observation_slot_count: int32 [128, 16], P('tile', 'member'), may hold values from 1 to 32
- local_radius: int32 [128, 16], P('tile', 'member'), may hold values from 16 to 128
- observed_value: float32 [128, 16, 32], P('tile', 'member'), may hold values from -9 to 9
- error_variance: float32 [128, 16, 32], P('tile', 'member'), may hold values from 0.25 to 2
Outputs:
- analysis: float32 [64, 128, 2048], P('member', 'tile')
All inputs are finite; a program needn't handle non-finite values.
Results may differ from a plain program's by a relative error of at most 0.0003.
Values sent between devices are 32-bit elements; how exact they have to be, the bound alone decides.
A program may use at most 128 MiB of HBM per device.

v0:
```python
import functools
import math

import jax
import jax.numpy as jnp
from jax import lax
from jax.experimental import pallas as pl
from jax.experimental.pallas import tpu as pltpu
from jax.sharding import PartitionSpec as P

COLS = 128
SWEEPS = 6
EDGE = 8
STRIP = 256
ROWS_PER_CHUNK = 16
PAIRS = 4


def split(x):
    high = x.astype(jnp.bfloat16)
    low = (x - high.astype(jnp.float32)).astype(jnp.bfloat16)
    return high, low


def product(a, b, dims=(((1,), (0,)), ((), ()))):
    dot = functools.partial(
        lax.dot_general, dimension_numbers=dims, preferred_element_type=jnp.float32
    )
    return dot(a[0], b[0]) + (dot(a[0], b[1]) + dot(a[1], b[0]))


def kernel(
    sizes,
    ensemble,
    velocity,
    columns_ref,
    count_ref,
    radius_ref,
    value_ref,
    variance_ref,
    out,
    extended,
    outgoing,
    gathered,
    analysed,
    column_lanes,
    weight_lanes,
    value_lanes,
    load_sem,
    halo_send,
    halo_recv,
    there_send,
    there_recv,
    there_own,
    back_send,
    back_recv,
    back_own,
):
    devices, bands, local, rows, width, step, slots = sizes
    members = devices * local
    chunks = rows // step
    me = lax.axis_index("member")
    band = lax.axis_index("tile")
    part = local * step
    body = pl.ds(COLS, width)

    loads = [
        pltpu.make_async_copy(
            ensemble, extended.at[pl.ds(0, local), pl.ds(EDGE, rows), body], load_sem.at[0]
        ),
        pltpu.make_async_copy(
            velocity, extended.at[pl.ds(local, 2), pl.ds(EDGE, rows), body], load_sem.at[1]
        ),
    ]
    for load in loads:
        load.start()

    barrier = pltpu.get_barrier_semaphore()

    @pl.loop(1, devices)
    def _(k):
        pl.semaphore_signal(barrier, inc=1, device_id={"member": lax.rem(me + k, devices)})

    @pl.when(band > 0)
    def _():
        pl.semaphore_signal(barrier, inc=1, device_id={"tile": band - 1})

    @pl.when(band < bands - 1)
    def _():
        pl.semaphore_signal(barrier, inc=1, device_id={"tile": band + 1})

    extended[:, :, 0:COLS] = jnp.zeros((local + 2, rows + 2 * EDGE, COLS), jnp.float32)
    extended[:, :, COLS + width :] = jnp.zeros((local + 2, rows + 2 * EDGE, COLS), jnp.float32)

    @pl.when(band == 0)
    def _():
        extended[:, 0:EDGE, COLS : COLS + width] = jnp.zeros((local + 2, EDGE, width), jnp.float32)

    @pl.when(band == bands - 1)
    def _():
        extended[:, EDGE + rows :, COLS : COLS + width] = jnp.zeros(
            (local + 2, EDGE, width), jnp.float32
        )

    def spread_lanes(x):
        return jnp.concatenate([x] * (COLS // slots), axis=1)

    lane = lax.broadcasted_iota(jnp.int32, (rows, COLS), 1)
    parity = lax.broadcasted_iota(jnp.int32, (rows, COLS), 0) % 2
    slot = lane % slots
    mine = (lane // slots) == parity
    columns = spread_lanes(columns_ref[...])
    live = mine & (slot < count_ref[...])
    offset = (columns.astype(jnp.float32) - 0.5 * (COLS - 1)) / radius_ref[...].astype(jnp.float32)
    weight = 1.0 / (1.0 + offset * offset) / spread_lanes(variance_ref[...])
    column_lanes[...] = jnp.where(mine, columns, -1)
    weight_lanes[...] = jnp.where(live, weight, 0.0)
    value_lanes[...] = jnp.where(mine, spread_lanes(value_ref[...]), 0.0)

    neighbours = (band > 0).astype(jnp.int32) + (band < bands - 1).astype(jnp.int32)
    pl.semaphore_wait(barrier, devices - 1 + neighbours)

    def halo(side):
        source, target, other = (
            (pl.ds(rows - EDGE, EDGE), pl.ds(0, EDGE), band + 1)
            if side == 0
            else (pl.ds(0, EDGE), pl.ds(EDGE + rows, EDGE), band - 1)
        )
        return [
            pltpu.make_async_remote_copy(
                src_ref=ref.at[:, source, :],
                dst_ref=extended.at[place, target, body],
                send_sem=halo_send.at[side, n],
                recv_sem=halo_recv.at[side, n],
                device_id={"tile": other},
            )
            for n, (ref, place) in enumerate(
                ((ensemble, pl.ds(0, local)), (velocity, pl.ds(local, 2)))
            )
        ]

    has = (band < bands - 1, band > 0)
    for side in range(2):

        @pl.when(has[side])
        def _():
            for copy in halo(side):
                copy.start()

    for load in loads:
        load.wait()

    window = step + 2 * EDGE
    reach = STRIP + 2 * COLS

    def forecast(c):
        first = pl.multiple_of(c * step, 8)

        @pl.loop(0, width // STRIP)
        def _(strip):
            lanes = pl.ds(pl.multiple_of(strip * STRIP, COLS), reach)
            span = pl.ds(first, window)
            u = extended[local, span, lanes]
            v = extended[local + 1, span, lanes]

            def nxt(x, axis):
                return pltpu.roll(x, x.shape[axis] - 1, axis)

            def prv(x, axis):
                return pltpu.roll(x, 1, axis)

            a = 0.5 * (u + nxt(u, 0))
            b = 0.5 * (v + nxt(v, 1))
            before_a, before_b = prv(a, 0), prv(b, 1)
            low_a, high_a = jnp.minimum(a, 0.0), jnp.maximum(before_a, 0.0)
            low_b, high_b = jnp.minimum(b, 0.0), jnp.maximum(before_b, 0.0)
            centre = (
                1.0
                - (jnp.maximum(a, 0.0) - jnp.minimum(before_a, 0.0))
                - (jnp.maximum(b, 0.0) - jnp.minimum(before_b, 0.0))
            )
            row = band * rows + c * step - EDGE + lax.broadcasted_iota(jnp.int32, u.shape, 0)
            col = strip * STRIP - COLS + lax.broadcasted_iota(jnp.int32, u.shape, 1)
            inside = (row >= 0) & (row < rows * bands) & (col >= 0) & (col < width)

            def substep(f):
                return (
                    centre * f
                    + (high_a * prv(f, 0) - low_a * nxt(f, 0))
                    + (high_b * prv(f, 1) - low_b * nxt(f, 1))
                )

            for m in range(local):
                f = extended[m, span, lanes]
                f = substep(jnp.where(inside, substep(f), 0.0))
                for h in range(STRIP // COLS):
                    outgoing[c, strip * (STRIP // COLS) + h, pl.ds(m * step, step), :] = f[
                        EDGE : EDGE + step, COLS * (1 + h) : COLS * (2 + h)
                    ]

        own = pltpu.make_async_copy(
            outgoing.at[c, me], gathered.at[c, pl.ds(me * part, part)], there_own.at[c]
        )
        own.start()

        @pl.loop(1, devices)
        def _(k):
            peer = lax.rem(me + k, devices)
            pltpu.make_async_remote_copy(
                src_ref=outgoing.at[c, peer],
                dst_ref=gathered.at[c, pl.ds(me * part, part)],
                send_sem=there_send.at[c],
                recv_sem=there_recv.at[c],
                device_id={"member": peer},
            ).start()

    @pl.loop(1, chunks - 1)
    def _(c):
        forecast(c)

    for side in range(2):

        @pl.when(has[1 - side])
        def _():
            for copy in halo(side):
                copy.wait_recv()

    @pl.loop(0, 2)
    def _(k):
        forecast(k * (chunks - 1))

    two = 2 * members
    row_index = lax.broadcasted_iota(jnp.int32, (two, two), 0)
    col_index = lax.broadcasted_iota(jnp.int32, (two, two), 1)
    identity = (row_index == col_index).astype(jnp.float32)
    upper = lax.broadcasted_iota(jnp.int32, (two, 1), 0) < members
    sublane = lax.broadcasted_iota(jnp.int32, (COLS, COLS), 0)
    across = (((1,), (1,)), ((), ()))

    def analyse(c, base):
        pairs = []
        for n in range(PAIRS):
            halves, seen, means, weight, value, averages = [], [], [], 0.0, 0.0, []
            for h in range(2):
                r = base + 2 * n + h
                tile_row = c * step + r
                x = gathered[c, pl.ds(r, members, stride=step), :]
                average = jnp.sum(x, axis=0, keepdims=True) * (1.0 / members)
                anomaly = x - average
                hit = (column_lanes[pl.ds(tile_row, 1), :] == sublane).astype(jnp.float32)
                hit = hit.astype(jnp.bfloat16)
                both = jnp.concatenate(
                    [anomaly, jnp.broadcast_to(average, (8, COLS))], axis=0
                )
                high, low = split(both)
                picked = jnp.dot(high, hit, preferred_element_type=jnp.float32) + jnp.dot(
                    low, hit, preferred_element_type=jnp.float32
                )
                halves.append(anomaly)
                averages.append(average)
                seen.append(picked[0:members])
                means.append(picked[members : members + 1])
                weight = weight + weight_lanes[pl.ds(tile_row, 1), :]
                value = value + value_lanes[pl.ds(tile_row, 1), :]
            spread = jnp.concatenate(seen, axis=0)
            scaled = spread * weight
            projected = jnp.sum(
                scaled * (value - (means[0] + means[1])), axis=1, keepdims=True
            )
            pairs.append((halves, averages, spread, scaled, projected))

        systems = [
            product(split(scaled), split(spread), across) + (members - 1.0) * identity
            for _, _, spread, scaled, _ in pairs
        ]
        norms = []
        for system in systems:
            squares = jnp.sum(system * system, axis=1, keepdims=True)
            norms.append(
                jnp.sqrt(
                    jnp.where(
                        upper,
                        jnp.sum(squares[0:members], axis=0, keepdims=True),
                        jnp.sum(squares[members:], axis=0, keepdims=True),
                    )
                )
            )
        roots = [system / norm for system, norm in zip(systems, norms)]
        inverses = [None] * PAIRS
        for sweep in range(SWEEPS):
            if sweep == 0:
                factors = [1.5 * identity - 0.5 * root for root in roots]
                inverses = factors
                parts = [split(factor) for factor in factors]
                inverse_parts = parts
                root_parts = [split(root) for root in roots]
            else:
                factors = [
                    1.5 * identity - 0.5 * product(z, y)
                    for z, y in zip(inverse_parts, root_parts)
                ]
                parts = [split(factor) for factor in factors]
                inverses = [product(p, z) for p, z in zip(parts, inverse_parts)]
                inverse_parts = [split(z) for z in inverses]
            if sweep < SWEEPS - 1:
                roots = [product(y, p) for y, p in zip(root_parts, parts)]
                root_parts = [split(y) for y in roots]
        for n in range(PAIRS):
            halves, averages, _, _, projected = pairs[n]
            inverse = inverses[n] * lax.rsqrt(norms[n])
            halfway = jnp.sum(inverse * projected, axis=0, keepdims=True)
            mean_weight = jnp.sum(inverse * halfway, axis=1, keepdims=True)
            anomaly = jnp.concatenate(halves, axis=0)
            moved = product(split(math.sqrt(members - 1.0) * inverse), split(anomaly))
            shift = mean_weight * anomaly
            for h in range(2):
                inner = slice(h * members, (h + 1) * members)
                centre = averages[h] + jnp.sum(shift[inner], axis=0, keepdims=True)
                analysed[c, pl.ds(base + 2 * n + h, members, stride=step), :] = (
                    moved[inner] + centre
                )

    def back(c, peer):
        return [
            pltpu.make_async_remote_copy(
                src_ref=analysed.at[c, pl.ds(peer * part + m * step, step)],
                dst_ref=out.at[
                    m,
                    pl.ds(pl.multiple_of(c * step, 8), step),
                    pl.ds(pl.multiple_of(me * COLS, COLS), COLS),
                ],
                send_sem=back_send.at[c],
                recv_sem=back_recv.at[c],
                device_id={"member": peer},
            )
            for m in range(local)
        ]

    def keep(c):
        return [
            pltpu.make_async_copy(
                analysed.at[c, pl.ds(me * part + m * step, step)],
                out.at[
                    m,
                    pl.ds(pl.multiple_of(c * step, 8), step),
                    pl.ds(pl.multiple_of(me * COLS, COLS), COLS),
                ],
                back_own.at[c, m],
            )
            for m in range(local)
        ]

    others = (devices - 1) * part

    def whole(ref, c, sem):
        piece = ref.at[c, pl.ds(0, others)]
        return pltpu.make_async_copy(piece, piece, sem.at[c])

    @pl.loop(0, chunks)
    def _(k):
        c = jnp.where(
            k < chunks - 2, k + 1, (k - (chunks - 2)) * (chunks - 1)
        )
        pltpu.make_async_copy(
            outgoing.at[c, me], gathered.at[c, pl.ds(me * part, part)], there_own.at[c]
        ).wait()
        whole(gathered, c, there_recv).wait()

        @pl.loop(0, step // (2 * PAIRS))
        def _(group):
            analyse(c, group * 2 * PAIRS)

        for copy in keep(c):
            copy.start()

        @pl.loop(1, devices)
        def _(j):
            for copy in back(c, lax.rem(me + j, devices)):
                copy.start()

    for side in range(2):

        @pl.when(has[side])
        def _():
            for copy in halo(side):
                copy.wait_send()

    @pl.loop(0, chunks)
    def _(c):
        whole(gathered, c, there_send).wait()
        whole(analysed, c, back_send).wait()
        for copy in keep(c):
            copy.wait()
        landed = out.at[
            :, pl.ds(pl.multiple_of(c * step, 8), step), pl.ds(0, (devices - 1) * COLS)
        ]
        pltpu.make_async_copy(landed, landed, back_recv.at[c]).wait()


def per_device(
    ensemble,
    velocity,
    observed_column,
    observation_slot_count,
    local_radius,
    observed_value,
    error_variance,
):
    devices, bands = lax.axis_size("member"), lax.axis_size("tile")
    local, rows, width = ensemble.shape
    slots = observed_column.shape[2]
    step = ROWS_PER_CHUNK
    chunks = rows // step
    part = local * step
    members = devices * local
    sizes = (devices, bands, local, rows, width, step, slots)
    vmem = pl.BlockSpec(memory_space=pltpu.VMEM)
    anywhere = pl.BlockSpec(memory_space=pl.ANY)
    dma = pltpu.SemaphoreType.DMA
    return pl.pallas_call(
        functools.partial(kernel, sizes),
        out_shape=jax.ShapeDtypeStruct(ensemble.shape, jnp.float32),
        in_specs=[anywhere] * 2 + [vmem] * 5,
        out_specs=anywhere,
        scratch_shapes=[
            pltpu.VMEM((local + 2, rows + 2 * EDGE, width + 2 * COLS), jnp.float32),
            pltpu.VMEM((chunks, devices, part, COLS), jnp.float32),
            pltpu.VMEM((chunks, members * step, COLS), jnp.float32),
            pltpu.VMEM((chunks, members * step, COLS), jnp.float32),
            pltpu.VMEM((rows, COLS), jnp.int32),
            pltpu.VMEM((rows, COLS), jnp.float32),
            pltpu.VMEM((rows, COLS), jnp.float32),
            dma((2,)),
            dma((2, 2)),
            dma((2, 2)),
            dma((chunks,)),
            dma((chunks,)),
            dma((chunks,)),
            dma((chunks,)),
            dma((chunks,)),
            dma((chunks, local)),
        ],
        compiler_params=pltpu.CompilerParams(
            collective_id=0, has_side_effects=True, vmem_limit_bytes=48 * 1024 * 1024
        ),
    )(
        ensemble,
        velocity,
        observed_column.reshape(rows, slots),
        observation_slot_count,
        local_radius,
        observed_value.reshape(rows, slots),
        error_variance.reshape(rows, slots),
    )


def solution(mesh):
    placed = (
        P("member", "tile", None),
        P(None, "tile", None),
        P("tile", "member", None),
        P("tile", "member"),
        P("tile", "member"),
        P("tile", "member", None),
        P("tile", "member", None),
    )
    return jax.shard_map(
        per_device, mesh=mesh, in_specs=placed, out_specs=P("member", "tile", None), check_vma=False
    )
```

profile of v0, /device:TPU:13, one launch (start us, length us, event | category | flops | bytes accessed | tf_op | source)
XLA Modules:
  0.0 107.2 jit_solution(11777850657498240470)
XLA Ops:
  0.0 0.8 copy.8
  0.8 0.7 copy.11.count_ref
  1.5 0.7 copy.12.radius_ref
  2.3 0.8 copy.9
  3.1 0.8 copy.10
  3.9 0.0 copy-start
  3.9 1.6 %copy-done = f32[4,64,2048]{2,1,0:T(8,128)S(1)} copy-done((f32[4,64,2048]{2,1,0:T(8,128)S(1)}, f32[4,64,2048]{2,1,0:T(8,128)}, u32[]{:S(2)}) %copy-start) | copy-done | bytes 2097176
  5.5 0.0 copy-start.1
  5.5 1.2 %copy-done.1 = f32[2,64,2048]{2,1,0:T(8,128)S(1)} copy-done((f32[2,64,2048]{2,1,0:T(8,128)S(1)}, f32[2,64,2048]{2,1,0:T(8,128)}, u32[]{:S(2)}) %copy-start.1) | copy-done | bytes 1048600
  6.7 99.1 %shard_map.73 = f32[4,64,2048]{2,1,0:T(8,128)S(1)} custom-call(f32[4,64,2048]{2,1,0:T(8,128)S(1)} %copy-done, f32[2,64,2048]{2,1,0:T(8,128)S(1)} %copy-done.1, s32[64,32]{1,0:T(8,128)S(1)} %bitcast.3, s32[64,1]{1,0:T(8,128)S(1)} %copy.11.count_ref, s32[64,1]{1,0:T(8,128)S(1)} %copy.12.radius_ref, f32[64,32]{1,0:T(8,128)S(1)} %bitcast.4, f32[64,32]{1,0:T(8,128)S(1)} %bitcast.5), custom_call_target="tpu_custom_call" | custom-call | tf_op jit(solution)/shard_map/pallas_call | solution.py:420
  105.8 1.3 %copy.14 = f32[4,64,2048]{2,1,0:T(8,128)} copy(f32[4,64,2048]{2,1,0:T(8,128)S(1)} %shard_map.73) | data formatting | bytes 4194304
Async XLA Ops:
  3.9 1.6 %copy-start = (f32[4,64,2048]{2,1,0:T(8,128)S(1)}, f32[4,64,2048]{2,1,0:T(8,128)}, u32[]{:S(2)}) copy-start(f32[4,64,2048]{2,1,0:T(8,128)} %ensemble.1) | copy-start | bytes 6291460
  5.5 1.2 %copy-start.1 = (f32[2,64,2048]{2,1,0:T(8,128)S(1)}, f32[2,64,2048]{2,1,0:T(8,128)}, u32[]{:S(2)}) copy-start(f32[2,64,2048]{2,1,0:T(8,128)} %velocity.1) | copy-start | bytes 3145732
where the time goes:
time: 108 us; the launch traced here: 107 us
  Pallas kernels  99.1 us (92%)
  local copies, waits for them, and re-layouts  8.02 us (7%)
    pallas_call x1, Pallas kernels, per_device(): pl.pallas_call(functools.partial(kernel, sizes), out_shape=jax.ShapeDtype...  99.1 us
    unnamed x10, local copies, waits for them, and re-layouts  8.02 us

commit v1 on v0

--- a/solution.py
+++ b/solution.py
@@ -102,21 +102,6 @@
             (local + 2, EDGE, width), jnp.float32
         )
 
-    def spread_lanes(x):
-        return jnp.concatenate([x] * (COLS // slots), axis=1)
-
-    lane = lax.broadcasted_iota(jnp.int32, (rows, COLS), 1)
-    parity = lax.broadcasted_iota(jnp.int32, (rows, COLS), 0) % 2
-    slot = lane % slots
-    mine = (lane // slots) == parity
-    columns = spread_lanes(columns_ref[...])
-    live = mine & (slot < count_ref[...])
-    offset = (columns.astype(jnp.float32) - 0.5 * (COLS - 1)) / radius_ref[...].astype(jnp.float32)
-    weight = 1.0 / (1.0 + offset * offset) / spread_lanes(variance_ref[...])
-    column_lanes[...] = jnp.where(mine, columns, -1)
-    weight_lanes[...] = jnp.where(live, weight, 0.0)
-    value_lanes[...] = jnp.where(mine, spread_lanes(value_ref[...]), 0.0)
-
     neighbours = (band > 0).astype(jnp.int32) + (band < bands - 1).astype(jnp.int32)
     pl.semaphore_wait(barrier, devices - 1 + neighbours)
 
@@ -150,14 +135,23 @@
     for load in loads:
         load.wait()
 
+    def far_first(n, place, count):
+        half = count // 2
+        near_base = (place // half) * half
+        base = jnp.where(n < half, half - near_base, near_base)
+        return base + lax.rem(place + n, half)
+
+    per_strip = STRIP // COLS
+    strips = width // STRIP
     window = step + 2 * EDGE
     reach = STRIP + 2 * COLS
 
     def forecast(c):
         first = pl.multiple_of(c * step, 8)
 
-        @pl.loop(0, width // STRIP)
-        def _(strip):
+        @pl.loop(0, strips)
+        def _(turn):
+            strip = far_first(turn, me // per_strip, strips)
             lanes = pl.ds(pl.multiple_of(strip * STRIP, COLS), reach)
             span = pl.ds(first, window)
             u = extended[local, span, lanes]
@@ -193,26 +187,29 @@
             for m in range(local):
                 f = extended[m, span, lanes]
                 f = substep(jnp.where(inside, substep(f), 0.0))
-                for h in range(STRIP // COLS):
-                    outgoing[c, strip * (STRIP // COLS) + h, pl.ds(m * step, step), :] = f[
+                for h in range(per_strip):
+                    outgoing[c, strip * per_strip + h, pl.ds(m * step, step), :] = f[
                         EDGE : EDGE + step, COLS * (1 + h) : COLS * (2 + h)
                     ]
 
-        own = pltpu.make_async_copy(
-            outgoing.at[c, me], gathered.at[c, pl.ds(me * part, part)], there_own.at[c]
-        )
-        own.start()
-
-        @pl.loop(1, devices)
-        def _(k):
-            peer = lax.rem(me + k, devices)
-            pltpu.make_async_remote_copy(
-                src_ref=outgoing.at[c, peer],
-                dst_ref=gathered.at[c, pl.ds(me * part, part)],
-                send_sem=there_send.at[c],
-                recv_sem=there_recv.at[c],
-                device_id={"member": peer},
-            ).start()
+            for h in range(per_strip):
+                peer = strip * per_strip + h
+
+                @pl.when(peer == me)
+                def _():
+                    pltpu.make_async_copy(
+                        outgoing.at[c, me], gathered.at[c, pl.ds(me * part, part)], there_own.at[c]
+                    ).start()
+
+                @pl.when(peer != me)
+                def _():
+                    pltpu.make_async_remote_copy(
+                        src_ref=outgoing.at[c, peer],
+                        dst_ref=gathered.at[c, pl.ds(me * part, part)],
+                        send_sem=there_send.at[c],
+                        recv_sem=there_recv.at[c],
+                        device_id={"member": peer},
+                    ).start()
 
     @pl.loop(1, chunks - 1)
     def _(c):
@@ -228,6 +225,30 @@
     @pl.loop(0, 2)
     def _(k):
         forecast(k * (chunks - 1))
+
+    def spread_lanes(x):
+        return jnp.concatenate([x] * (COLS // slots), axis=1)
+
+    lane = lax.broadcasted_iota(jnp.int32, (rows, COLS), 1)
+    parity = lax.broadcasted_iota(jnp.int32, (rows, COLS), 0) % 2
+    slot = lane % slots
+    mine = (lane // slots) == parity
+    columns = spread_lanes(columns_ref[...].T)
+    square = (rows, rows)
+    diagonal = lax.broadcasted_iota(jnp.int32, square, 0) == lax.broadcasted_iota(
+        jnp.int32, square, 1
+    )
+
+    def upright(ref):
+        line = jnp.broadcast_to(ref[...].astype(jnp.float32), square)
+        return jnp.sum(jnp.where(diagonal, line, 0.0), axis=1, keepdims=True)
+
+    live = mine & (slot.astype(jnp.float32) < upright(count_ref))
+    offset = (columns.astype(jnp.float32) - 0.5 * (COLS - 1)) / upright(radius_ref)
+    weight = 1.0 / (1.0 + offset * offset) / spread_lanes(variance_ref[...].T)
+    column_lanes[...] = jnp.where(mine, columns, -1)
+    weight_lanes[...] = jnp.where(live, weight, 0.0)
+    value_lanes[...] = jnp.where(mine, spread_lanes(value_ref[...].T), 0.0)
 
     two = 2 * members
     row_index = lax.broadcasted_iota(jnp.int32, (two, two), 0)
@@ -373,10 +394,14 @@
         for copy in keep(c):
             copy.start()
 
-        @pl.loop(1, devices)
-        def _(j):
-            for copy in back(c, lax.rem(me + j, devices)):
-                copy.start()
+        @pl.loop(0, devices)
+        def _(turn):
+            peer = far_first(turn, me, devices)
+
+            @pl.when(peer != me)
+            def _():
+                for copy in back(c, peer):
+                    copy.start()
 
     for side in range(2):
 
@@ -441,16 +466,16 @@
             dma((chunks, local)),
         ],
         compiler_params=pltpu.CompilerParams(
-            collective_id=0, has_side_effects=True, vmem_limit_bytes=48 * 1024 * 1024
+            collective_id=0, has_side_effects=True, vmem_limit_bytes=62 * 1024 * 1024
         ),
     )(
         ensemble,
         velocity,
-        observed_column.reshape(rows, slots),
-        observation_slot_count,
-        local_radius,
-        observed_value.reshape(rows, slots),
-        error_variance.reshape(rows, slots),
+        observed_column.reshape(rows, slots).T,
+        observation_slot_count.reshape(1, rows),
+        local_radius.reshape(1, rows),
+        observed_value.reshape(rows, slots).T,
+        error_variance.reshape(rows, slots).T,
     )
 
 

time: 108 us -> 102 us (0.944)
  the two profiles are of different devices: /device:TPU:13 before, /device:TPU:0 now
where the time goes in v1:
time: 102 us
  Pallas kernels  99.1 us (97%)
  local copies, waits for them, and re-layouts  3.14 us (3%)
    pallas_call x1, Pallas kernels, per_device(): pl.pallas_call(functools.partial(kernel, sizes), out_shape=jax.ShapeDtype...  99.1 us
    unnamed x1, local copies, waits for them, and re-layouts  3.14 us

profile of v1, /device:TPU:0, one launch (start us, length us, event | category | flops | bytes accessed | tf_op | source)
XLA Modules:
  0.0 102.2 jit_solution(5214687287439449185)
XLA Ops:
  0.0 99.1 %shard_map.73 = f32[4,64,2048]{2,1,0:T(8,128)} custom-call(f32[4,64,2048]{2,1,0:T(8,128)} %ensemble.1, f32[2,64,2048]{2,1,0:T(8,128)} %velocity.1, s32[32,64]{1,0:T(8,128)} %bitcast.11, s32[1,64]{1,0:T(1,128)} %bitcast.14, s32[1,64]{1,0:T(1,128)} %bitcast.15, f32[32,64]{1,0:T(8,128)} %bitcast.12, f32[32,64]{1,0:T(8,128)} %bitcast.13), custom_call_target="tpu_custom_call" | custom-call | tf_op jit(solution)/shard_map/pallas_call | solution.py:445
  99.1 3.1 %copy.9 = f32[4,64,2048]{2,1,0:T(8,128)} copy(f32[4,64,2048]{2,1,0:T(8,128)} %shard_map.73) | data formatting | bytes 4194304

commit v2 on v1

--- a/solution.py
+++ b/solution.py
@@ -341,13 +341,21 @@
                     moved[inner] + centre
                 )
 
-    def back(c, peer):
+    group_rows = 2 * PAIRS
+
+    def back(c, group, peer):
         return [
             pltpu.make_async_remote_copy(
-                src_ref=analysed.at[c, pl.ds(peer * part + m * step, step)],
+                src_ref=analysed.at[
+                    c,
+                    pl.ds(
+                        pl.multiple_of(peer * part + m * step + group * group_rows, 8),
+                        group_rows,
+                    ),
+                ],
                 dst_ref=out.at[
                     m,
-                    pl.ds(pl.multiple_of(c * step, 8), step),
+                    pl.ds(pl.multiple_of(c * step + group * group_rows, 8), group_rows),
                     pl.ds(pl.multiple_of(me * COLS, COLS), COLS),
                 ],
                 send_sem=back_send.at[c],
@@ -387,21 +395,21 @@
         ).wait()
         whole(gathered, c, there_recv).wait()
 
-        @pl.loop(0, step // (2 * PAIRS))
+        @pl.loop(0, step // group_rows)
         def _(group):
-            analyse(c, group * 2 * PAIRS)
+            analyse(c, group * group_rows)
+
+            @pl.loop(0, devices)
+            def _(turn):
+                peer = far_first(turn, me, devices)
+
+                @pl.when(peer != me)
+                def _():
+                    for copy in back(c, group, peer):
+                        copy.start()
 
         for copy in keep(c):
             copy.start()
-
-        @pl.loop(0, devices)
-        def _(turn):
-            peer = far_first(turn, me, devices)
-
-            @pl.when(peer != me)
-            def _():
-                for copy in back(c, peer):
-                    copy.start()
 
     for side in range(2):
 

time: 102 us -> 102 us (level)
  no operation moved by 1% of the time
where the time goes in v2:
time: 102 us
  Pallas kernels  99.1 us (97%)
  local copies, waits for them, and re-layouts  3.14 us (3%)
    pallas_call x1, Pallas kernels, per_device(): pl.pallas_call(functools.partial(kernel, sizes), out_shape=jax.ShapeDtype...  99.1 us
    unnamed x1, local copies, waits for them, and re-layouts  3.14 us

profile of v2, /device:TPU:0, one launch (start us, length us, event | category | flops | bytes accessed | tf_op | source)
XLA Modules:
  0.0 102.2 jit_solution(8917463197344166328)
XLA Ops:
  0.0 99.1 %shard_map.73 = f32[4,64,2048]{2,1,0:T(8,128)} custom-call(f32[4,64,2048]{2,1,0:T(8,128)} %ensemble.1, f32[2,64,2048]{2,1,0:T(8,128)} %velocity.1, s32[32,64]{1,0:T(8,128)} %bitcast.11, s32[1,64]{1,0:T(1,128)} %bitcast.14, s32[1,64]{1,0:T(1,128)} %bitcast.15, f32[32,64]{1,0:T(8,128)} %bitcast.12, f32[32,64]{1,0:T(8,128)} %bitcast.13), custom_call_target="tpu_custom_call" | custom-call | tf_op jit(solution)/shard_map/pallas_call | solution.py:453
  99.1 3.1 %copy.9 = f32[4,64,2048]{2,1,0:T(8,128)} copy(f32[4,64,2048]{2,1,0:T(8,128)} %shard_map.73) | data formatting | bytes 4194304

commit v3 on v2

--- a/solution.py
+++ b/solution.py
@@ -430,6 +430,27 @@
         pltpu.make_async_copy(landed, landed, back_recv.at[c]).wait()
 
 
+def place(source, out, staged, in_sem, out_sem):
+    local, rows, _ = source.shape
+    piece = rows // 2
+    spots = [(m, pl.ds(h * piece, piece)) for m in range(local) for h in range(2)]
+    reads = [
+        pltpu.make_async_copy(source.at[spot], staged.at[spot], in_sem.at[n])
+        for n, spot in enumerate(spots)
+    ]
+    writes = [
+        pltpu.make_async_copy(staged.at[spot], out.at[spot], out_sem.at[n])
+        for n, spot in enumerate(spots)
+    ]
+    for read in reads:
+        read.start()
+    for read, write in zip(reads, writes):
+        read.wait()
+        write.start()
+    for write in writes:
+        write.wait()
+
+
 def per_device(
     ensemble,
     velocity,
@@ -450,7 +471,7 @@
     vmem = pl.BlockSpec(memory_space=pltpu.VMEM)
     anywhere = pl.BlockSpec(memory_space=pl.ANY)
     dma = pltpu.SemaphoreType.DMA
-    return pl.pallas_call(
+    analysis = pl.pallas_call(
         functools.partial(kernel, sizes),
         out_shape=jax.ShapeDtypeStruct(ensemble.shape, jnp.float32),
         in_specs=[anywhere] * 2 + [vmem] * 5,
@@ -485,6 +506,18 @@
         observed_value.reshape(rows, slots).T,
         error_variance.reshape(rows, slots).T,
     )
+    return pl.pallas_call(
+        place,
+        out_shape=jax.ShapeDtypeStruct(ensemble.shape, jnp.float32),
+        in_specs=[anywhere],
+        out_specs=anywhere,
+        scratch_shapes=[
+            pltpu.VMEM(ensemble.shape, jnp.float32),
+            dma((2 * local,)),
+            dma((2 * local,)),
+        ],
+        compiler_params=pltpu.CompilerParams(vmem_limit_bytes=62 * 1024 * 1024),
+    )(analysis)
 
 
 def solution(mesh):

time: 102 us -> 102 us (level)
  local copies, waits for them, and re-layouts: 3.14 us -> 0 us
  Pallas kernels: 99.1 us -> 101 us
    unnamed x1 -> x0, local copies, waits for them, and re-layouts: 3.14 us -> none
    pallas_call x0 -> x1, Pallas kernels: none -> 2.39 us  [per_device(): pl.pallas_call(place, out_shape=jax.ShapeDtypeStruct(ensemble.shape, jnp....]
where the time goes in v3:
time: 102 us; the launch traced here: 101 us
  Pallas kernels  101 us (99%)
    pallas_call x1, Pallas kernels, per_device(): pl.pallas_call(functools.partial(kernel, sizes), out_shape=jax.ShapeDtype...  99.1 us
    pallas_call x1, Pallas kernels, per_device(): pl.pallas_call(place, out_shape=jax.ShapeDtypeStruct(ensemble.shape, jnp....  2.39 us

profile of v3, /device:TPU:0, one launch (start us, length us, event | category | flops | bytes accessed | tf_op | source)
XLA Modules:
  0.0 101.5 jit_solution(14953889722423933807)
XLA Ops:
  0.0 99.1 %shard_map.73.source = f32[4,64,2048]{2,1,0:T(8,128)} custom-call(f32[4,64,2048]{2,1,0:T(8,128)} %ensemble.1, f32[2,64,2048]{2,1,0:T(8,128)} %velocity.1, s32[32,64]{1,0:T(8,128)} %bitcast.11, s32[1,64]{1,0:T(1,128)} %bitcast.14, s32[1,64]{1,0:T(1,128)} %bitcast.15, f32[32,64]{1,0:T(8,128)} %bitcast.12, f32[32,64]{1,0:T(8,128)} %bitcast.13), custom_call_target="tpu_custom_call" | custom-call | tf_op jit(solution)/shard_map/pallas_call | solution.py:474
  99.1 2.4 %shard_map.74 = f32[4,64,2048]{2,1,0:T(8,128)} custom-call(f32[4,64,2048]{2,1,0:T(8,128)} %shard_map.73.source), custom_call_target="tpu_custom_call" | custom-call | tf_op jit(solution)/shard_map/pallas_call | solution.py:509

commit v4 on v3

--- a/solution.py
+++ b/solution.py
@@ -12,7 +12,7 @@
 SWEEPS = 6
 EDGE = 8
 STRIP = 256
-ROWS_PER_CHUNK = 16
+ROWS_PER_CHUNK = 8
 PAIRS = 4
 
 

time: 102 us -> 102 us (level)
  no operation moved by 1% of the time
where the time goes in v4:
time: 102 us
  Pallas kernels  102 us (100%)
    pallas_call x1, Pallas kernels, per_device(): pl.pallas_call(functools.partial(kernel, sizes), out_shape=jax.ShapeDtype...  99.3 us
    pallas_call x1, Pallas kernels, per_device(): pl.pallas_call(place, out_shape=jax.ShapeDtypeStruct(ensemble.shape, jnp....  2.39 us

profile of v4, /device:TPU:0, one launch (start us, length us, event | category | flops | bytes accessed | tf_op | source)
XLA Modules:
  0.0 101.7 jit_solution(7567323180490084085)
XLA Ops:
  0.0 99.3 %shard_map.73.source = f32[4,64,2048]{2,1,0:T(8,128)} custom-call(f32[4,64,2048]{2,1,0:T(8,128)} %ensemble.1, f32[2,64,2048]{2,1,0:T(8,128)} %velocity.1, s32[32,64]{1,0:T(8,128)} %bitcast.11, s32[1,64]{1,0:T(1,128)} %bitcast.14, s32[1,64]{1,0:T(1,128)} %bitcast.15, f32[32,64]{1,0:T(8,128)} %bitcast.12, f32[32,64]{1,0:T(8,128)} %bitcast.13), custom_call_target="tpu_custom_call" | custom-call | tf_op jit(solution)/shard_map/pallas_call | solution.py:474
  99.4 2.4 %shard_map.74 = f32[4,64,2048]{2,1,0:T(8,128)} custom-call(f32[4,64,2048]{2,1,0:T(8,128)} %shard_map.73.source), custom_call_target="tpu_custom_call" | custom-call | tf_op jit(solution)/shard_map/pallas_call | solution.py:509
